TPU v7x, 32 devices: a whole 2x2x4 slice. The times are simulated.
32 devices in a mesh: vin: 8 (over z, core), vout: 2 (over x), cell: 2 (over y).
Axes of the slice: x: 2, y: 2, z: 4, core: 2. Of those that a mesh axis runs over, the one named last changes fastest.
Arguments:
- distribution: bfloat16 [8, 13824, 4, 128], P('vout', 'vin', 'cell'), may hold values from -6 to 6
- collision: bfloat16 [13824, 13824], P('vout', 'vin'), may hold values from -1 to 3
- speeds: float32 [3, 13824], P(None, 'vout'), may hold values from 0.05 to 0.3
- directions: int32 [3, 13824], P(None, 'vout'), may hold values from 0 to 1
- cell_flags: int32 [8, 4, 128], P('vin', 'cell'), may hold values 0 or 1
Outputs:
- updated: bfloat16 [8, 13824, 4, 128], P('vin', 'vout', 'cell')
Inputs may be any that keep to these rules, and one draw needn't show every extreme that they name: `directions`: 1 means the component is positive, 0 negative. `cell_flags`: 1 marks a solid cell, where nothing is transported.
All inputs are finite; a program needn't handle non-finite values. No bound on the sum of `cell_flags` on one device may be relied on, other than what follows from the above.
Results may differ from a plain program's by a relative error of at most 0.023.
Values may be sent and summed in bfloat16 or wider, within the bound.
A program may use at most 128 MiB of HBM per device.

v0:
```python
import jax
import jax.numpy as jnp
from jax import lax
from jax.sharding import PartitionSpec as P

CHUNKS = 4


def from_lower(values, axis):
    ends = lax.axis_size(axis) - 1
    return lax.ppermute(values, axis, [(i, i + 1) for i in range(ends)])


def from_higher(values, axis):
    ends = lax.axis_size(axis) - 1
    return lax.ppermute(values, axis, [(i + 1, i) for i in range(ends)])


def shifted(values, step):
    edge = jnp.zeros_like(values[:, :1])
    if step > 0:
        return jnp.concatenate([edge, values[:, :-1]], axis=1)
    return jnp.concatenate([values[:, 1:], edge], axis=1)


def transport(center, neighbours, speeds, positive, fluid):
    middle = center.astype(jnp.float32)
    flux = jnp.zeros_like(middle)
    for component, (low, high) in enumerate(neighbours):
        upstream = jnp.where(positive[component][:, None], low, high).astype(jnp.float32)
        flux = flux + speeds[component][:, None] * (middle - upstream)
    return (middle - fluid[None, :] * flux).astype(jnp.bfloat16)


def on_device(distribution, collision, speeds, directions, cell_flags):
    rows = distribution.shape[2]
    velocities = collision.shape[0]
    chunk = velocities // CHUNKS
    planes = [
        lax.all_gather(distribution[:, :, row, :], "vout", axis=0, tiled=True)
        for row in range(rows)
    ]
    fluid = (1 - cell_flags[0]).astype(jnp.float32)
    relaxed = [[None] * rows for _ in range(CHUNKS)]
    for row in range(rows):
        for part in range(CHUNKS):
            block = lax.slice_in_dim(collision, part * chunk, (part + 1) * chunk, axis=0)
            partial = jnp.einsum(
                "vu,zux->zvx", block, planes[row], preferred_element_type=jnp.float32
            ).astype(jnp.bfloat16)
            relaxed[part][row] = lax.psum_scatter(partial, "vin", scatter_dimension=0, tiled=True)[
                0
            ]
    outs = []
    for part in range(CHUNKS):
        cells = relaxed[part]
        own = slice(part * chunk, (part + 1) * chunk)
        positive = directions[:, own] == 1
        pace = speeds[:, own]
        before = from_lower(cells[-1], "cell")
        after = from_higher(cells[0], "cell")
        column = [before, *cells, after]
        done = []
        for row in range(rows):
            center = cells[row]
            neighbours = (
                (shifted(center, 1), shifted(center, -1)),
                (column[row], column[row + 2]),
                (from_lower(center, "vin"), from_higher(center, "vin")),
            )
            done.append(transport(center, neighbours, pace, positive, fluid[row]))
        outs.append(jnp.stack(done, axis=1))
    return jnp.concatenate(outs, axis=0)[None]


def solution(mesh):
    return jax.shard_map(
        on_device,
        mesh=mesh,
        in_specs=(
            P("vout", "vin", "cell", None),
            P("vout", "vin"),
            P(None, "vout"),
            P(None, "vout"),
            P("vin", "cell", None),
        ),
        out_specs=P("vin", "vout", "cell", None),
        check_vma=False,
    )
```

profile of v0, /device:TPU:13, one launch (start us, length us, event | category | flops | bytes accessed | tf_op | source)
XLA Modules:
  0.0 619.9 jit_solution(6708715030905493566)
XLA Ops:
  6.5 7.7 %fusion.160 = (bf16[4,1728,1,128]{3,2,1,0:T(2,128)(2,1)S(1)}, bf16[4,1728,1,128]{3,2,1,0:T(2,128)(2,1)S(1)}) fusion(bf16[4,1728,2,128]{3,2,1,0:T(2,128)(2,1)} %param.5), kind=kLoop, calls=%fused_computation.176 | loop fusion | bytes 7077888 | tf_op jit(solution)/shard_map/slice | solution.py:40
  17.3 49.0 %all-gather.7.cloned.1.call-done = bf16[8,1728,1,128]{3,1,2,0:T(8,128)(2,1)} async-done(((bf16[4,1728,1,128]{3,1,2,0:T(8,128)(2,1)}), bf16[8,1728,1,128]{3,1,2,0:T(8,128)(2,1)}) %all-gather.7.cloned.1.call-update) | async-done | bytes 3538960 | tf_op jit(solution)/shard_map/all_gather | solution.py:40
  66.3 14.6 %fusion.56 = bf16[8,1728,128]{2,1,0:T(8,128)(2,1)} fusion(bf16[8,1728,1,128]{3,1,2,0:T(8,128)(2,1)} %all-gather.7.cloned.1.call-done, bf16[6912,1728]{0,1:T(8,128)(2,1)} %param.6), kind=kOutput, calls=%fused_computation.41 | convolution fusion | flops 6117064704 | bytes 13271040 | tf_op jit(solution)/shard_map/vu,zux->zvx/dot_general | solution.py:48
  81.0 36.3 %all-gather.5.cloned.1.call-done = bf16[8,1728,1,128]{3,1,2,0:T(8,128)(2,1)} async-done(((bf16[4,1728,1,128]{3,1,2,0:T(8,128)(2,1)}), bf16[8,1728,1,128]{3,1,2,0:T(8,128)(2,1)}) %all-gather.5.cloned.1.call-update) | async-done | bytes 3538960 | tf_op jit(solution)/shard_map/all_gather | solution.py:40
  117.2 14.6 %fusion.61 = bf16[8,1728,128]{2,1,0:T(8,128)(2,1)} fusion(bf16[8,1728,1,128]{3,1,2,0:T(8,128)(2,1)} %all-gather.5.cloned.1.call-done, bf16[6912,1728]{0,1:T(8,128)(2,1)} %param.6), kind=kOutput, calls=%fused_computation.42 | convolution fusion | flops 6117064704 | bytes 13271040 | tf_op jit(solution)/shard_map/vu,zux->zvx/dot_general | solution.py:48
  133.9 10.8 %fusion.66 = bf16[8,1728,128]{2,1,0:T(8,128)(2,1)} fusion(bf16[8,1728,1,128]{3,1,2,0:T(8,128)(2,1)S(1)} %copy-done.43, bf16[6912,1728]{0,1:T(8,128)(2,1)} %param.6), kind=kOutput, calls=%fused_computation.43 | convolution fusion | flops 6117064704 | bytes 13271040 | tf_op jit(solution)/shard_map/vu,zux->zvx/dot_general | solution.py:48
  144.8 11.5 %fusion.71 = bf16[8,1728,128]{2,1,0:T(8,128)(2,1)} fusion(bf16[8,1728,1,128]{3,1,2,0:T(8,128)(2,1)} %all-gather.5.cloned.1.call-done, bf16[6912,1728]{0,1:T(8,128)(2,1)} %param.6), kind=kOutput, calls=%fused_computation.44 | convolution fusion | flops 6117064704 | bytes 13271040 | tf_op jit(solution)/shard_map/vu,zux->zvx/dot_general | solution.py:48
  156.4 14.2 %fusion.76 = bf16[8,1728,128]{2,1,0:T(8,128)(2,1)} fusion(bf16[8,1728,1,128]{3,1,2,0:T(8,128)(2,1)S(1)} %copy-done.43, bf16[6912,1728]{0,1:T(8,128)(2,1)} %param.6), kind=kOutput, calls=%fused_computation.45 | convolution fusion | flops 6117064704 | bytes 13271040 | tf_op jit(solution)/shard_map/vu,zux->zvx/dot_general | solution.py:48
  170.9 14.7 %fusion.81 = bf16[8,1728,128]{2,1,0:T(8,128)(2,1)} fusion(bf16[8,1728,1,128]{3,1,2,0:T(8,128)(2,1)} %all-gather.5.cloned.1.call-done, bf16[6912,1728]{0,1:T(8,128)(2,1)} %param.6), kind=kOutput, calls=%fused_computation.46 | convolution fusion | flops 6117064704 | bytes 13271040 | tf_op jit(solution)/shard_map/vu,zux->zvx/dot_general | solution.py:48
  185.7 10.9 %fusion.86 = bf16[8,1728,128]{2,1,0:T(8,128)(2,1)} fusion(bf16[8,1728,1,128]{3,1,2,0:T(8,128)(2,1)S(1)} %copy-done.43, bf16[6912,1728]{0,1:T(8,128)(2,1)} %param.6), kind=kOutput, calls=%fused_computation.47 | convolution fusion | flops 6117064704 | bytes 13271040 | tf_op jit(solution)/shard_map/vu,zux->zvx/dot_general | solution.py:48
  196.6 2.0 copy-done.44
  198.6 10.9 %fusion.91 = bf16[8,1728,128]{2,1,0:T(8,128)(2,1)} fusion(bf16[8,1728,1,128]{3,1,2,0:T(8,128)(2,1)S(1)} %copy-done.44, bf16[6912,1728]{0,1:T(8,128)(2,1)} %param.6), kind=kOutput, calls=%fused_computation.48 | convolution fusion | flops 6117064704 | bytes 13271040 | tf_op jit(solution)/shard_map/vu,zux->zvx/dot_general | solution.py:48
  214.6 3.7 collective-permute-start.22
  218.4 1.9 collective-permute-start.23
  220.3 2.9 collective-permute-start.21
  223.3 3.9 collective-permute-start.19
  227.2 2.3 collective-permute-start.20
  229.5 2.2 fusion.168
  231.8 2.3 fusion.167
  234.0 26.6 %reduce-scatter.19.cloned.1.call-done = bf16[1,1728,128]{2,1,0:T(8,128)(2,1)} async-done(((bf16[8,1728,128]{2,1,0:T(8,128)(2,1)}), bf16[1,1728,128]{2,1,0:T(8,128)(2,1)}) %reduce-scatter.19.cloned.1.call-update) | async-done | bytes 442384 | tf_op jit(solution)/shard_map/reduce_scatter | solution.py:51
  260.6 2.2 fusion.166
  262.8 42.4 %reduce-scatter.17.cloned.1.call-done = bf16[1,1728,128]{2,1,0:T(8,128)(2,1)} async-done(((bf16[8,1728,128]{2,1,0:T(8,128)(2,1)}), bf16[1,1728,128]{2,1,0:T(8,128)(2,1)}) %reduce-scatter.17.cloned.1.call-update) | async-done | bytes 442384 | tf_op jit(solution)/shard_map/reduce_scatter | solution.py:51
  305.2 2.2 fusion.165
  307.5 42.4 %reduce-scatter.15.cloned.1.call-done = bf16[1,1728,128]{2,1,0:T(8,128)(2,1)} async-done(((bf16[8,1728,128]{2,1,0:T(8,128)(2,1)}), bf16[1,1728,128]{2,1,0:T(8,128)(2,1)}) %reduce-scatter.15.cloned.1.call-update) | async-done | bytes 442384 | tf_op jit(solution)/shard_map/reduce_scatter | solution.py:51
  349.9 2.3 fusion.164
  352.2 42.5 %reduce-scatter.13.cloned.1.call-done = bf16[1,1728,128]{2,1,0:T(8,128)(2,1)} async-done(((bf16[8,1728,128]{2,1,0:T(8,128)(2,1)}), bf16[1,1728,128]{2,1,0:T(8,128)(2,1)}) %reduce-scatter.13.cloned.1.call-update) | async-done | bytes 442384 | tf_op jit(solution)/shard_map/reduce_scatter | solution.py:51
  396.1 43.3 %reduce-scatter.11.cloned.1.call-done = bf16[1,1728,128]{2,1,0:T(8,128)(2,1)} async-done(((bf16[8,1728,128]{2,1,0:T(8,128)(2,1)}), bf16[1,1728,128]{2,1,0:T(8,128)(2,1)}) %reduce-scatter.11.cloned.1.call-update) | async-done | bytes 442384 | tf_op jit(solution)/shard_map/reduce_scatter | solution.py:51
  440.8 43.2 %reduce-scatter.9.cloned.1.call-done = bf16[1,1728,128]{2,1,0:T(8,128)(2,1)} async-done(((bf16[8,1728,128]{2,1,0:T(8,128)(2,1)}), bf16[1,1728,128]{2,1,0:T(8,128)(2,1)}) %reduce-scatter.9.cloned.1.call-update) | async-done | bytes 442384 | tf_op jit(solution)/shard_map/reduce_scatter | solution.py:51
  486.8 2.4 collective-permute-start.16
  491.3 4.7 fusion.152
  496.0 4.3 collective-permute-start.15
  500.3 3.9 collective-permute-start.13
  506.3 4.4 fusion.153
  512.0 3.6 collective-permute-start.10
  517.8 2.2 fusion.154
  520.0 4.3 collective-permute-start.9
  524.4 3.9 collective-permute-start.7
  530.3 2.2 fusion.155
  533.8 3.6 collective-permute-start.4
  539.5 2.2 fusion.156
  541.7 4.3 collective-permute-start.3
  546.1 3.9 collective-permute-start.1
  551.9 2.2 fusion.157
  555.8 2.2 fusion.158
  559.9 8.1 %collective-permute-done = bf16[1728,128]{1,0:T(8,128)(2,1)S(1)} collective-permute-done((bf16[1728,128]{1,0:T(8,128)(2,1)S(1)}, bf16[1728,128]{1,0:T(8,128)(2,1)S(1)}, u32[]{:S(2)}, u32[]{:S(2)}) %collective-permute-start) | collective-permute-done | bytes 442400 | tf_op jit(solution)/shard_map/ppermute | solution.py:11
  568.1 2.2 fusion.159
  570.2 12.5 %maximum_bitcast_fusion = bf16[1,6912,2,128]{3,1,2,0:T(8,128)(2,1)S(1)} fusion(bf16[1728,1,128]{2,0,1:T(8,128)(2,1)S(1)} %fusion.152, bf16[1728,1,128]{2,0,1:T(8,128)(2,1)S(1)} %fusion.153, bf16[1728,1,128]{2,0,1:T(8,128)(2,1)S(1)} %fusion.154, bf16[1728,1,128]{2,0,1:T(8,128)(2,1)S(1)} %fusion.155, bf16[1728,1,128]{2,0,1:T(8,128)(2,1)S(1)} %fusion.156, ...), kind=kLoop, calls=%fused_computation.32 | loop fusion | flops 28311552 | bytes 7077888 | tf_op jit(solution)/shard_map/broadcast_in_dim | solution.py:73
  582.8 30.0 %copy.19 = bf16[1,6912,2,128]{3,2,1,0:T(2,128)(2,1)} copy(bf16[1,6912,2,128]{3,1,2,0:T(8,128)(2,1)S(1)} %maximum_bitcast_fusion) | data formatting | bytes 7077888 | tf_op jit(solution)/shard_map/broadcast_in_dim | solution.py:73
  (157 shorter events, 34.1 us)
Async XLA Ops:
  6.5 59.8 %all-gather.7.cloned.1.call-start = ((), (), s32[]{:S(2)}) async-start(), calls=%async_computation.17 | async-start | bytes 5308416 | tf_op jit(solution)/shard_map/all_gather | solution.py:40
  15.7 101.6 %all-gather.5.cloned.1.call-start = ((), (), s32[]{:S(2)}) async-start(), calls=%async_computation.16 | async-start | bytes 5308416 | tf_op jit(solution)/shard_map/all_gather | solution.py:40
  17.2 197.4 %reduce-scatter.23.cloned.1.call-start = ((), (), s32[]{:S(2)}) async-start(), calls=%async_computation.15 | async-start | bytes 3981312 | tf_op jit(solution)/shard_map/reduce_scatter | solution.py:51
  80.9 139.4 %reduce-scatter.21.cloned.1.call-start = ((), (), s32[]{:S(2)}) async-start(), calls=%async_computation.14 | async-start | bytes 3981312 | tf_op jit(solution)/shard_map/reduce_scatter | solution.py:51
  131.9 128.7 %reduce-scatter.19.cloned.1.call-start = ((), (), s32[]{:S(2)}) async-start(), calls=%async_computation.13 | async-start | bytes 3981312 | tf_op jit(solution)/shard_map/reduce_scatter | solution.py:51
  144.8 160.4 %reduce-scatter.17.cloned.1.call-start = ((), (), s32[]{:S(2)}) async-start(), calls=%async_computation.12 | async-start | bytes 3981312 | tf_op jit(solution)/shard_map/reduce_scatter | solution.py:51
  156.4 193.5 %reduce-scatter.15.cloned.1.call-start = ((), (), s32[]{:S(2)}) async-start(), calls=%async_computation.11 | async-start | bytes 3981312 | tf_op jit(solution)/shard_map/reduce_scatter | solution.py:51
  170.6 224.0 %reduce-scatter.13.cloned.1.call-start = ((), (), s32[]{:S(2)}) async-start(), calls=%async_computation.10 | async-start | bytes 3981312 | tf_op jit(solution)/shard_map/reduce_scatter | solution.py:51
  185.6 253.8 %reduce-scatter.11.cloned.1.call-start = ((), (), s32[]{:S(2)}) async-start(), calls=%async_computation.9 | async-start | bytes 3981312 | tf_op jit(solution)/shard_map/reduce_scatter | solution.py:51
  196.6 287.4 %reduce-scatter.9.cloned.1.call-start = ((), (), s32[]{:S(2)}) async-start(), calls=%async_computation.8 | async-start | bytes 3981312 | tf_op jit(solution)/shard_map/reduce_scatter | solution.py:51
  214.6 270.8 %collective-permute-start.22 = (bf16[1728,128]{1,0:T(8,128)(2,1)}, bf16[1728,128]{1,0:T(8,128)(2,1)}, u32[]{:S(2)}, u32[]{:S(2)}) collective-permute-start(bf16[1728,128]{1,0:T(8,128)(2,1)} %bitcast.180), channel_id=1, source_target_pairs={{0,4},{4,8},{8,12},{12,16},{16,20},{20,24},{24,28},{1,5},{5,9},{9,... | collective-permute-start | bytes 1327112 | tf_op jit(solution)/shard_map/ppermute | solution.py:11
  218.4 268.4 %collective-permute-start.23 = (bf16[1728,128]{1,0:T(8,128)(2,1)}, bf16[1728,128]{1,0:T(8,128)(2,1)}, u32[]{:S(2)}, u32[]{:S(2)}) collective-permute-start(bf16[1728,128]{1,0:T(8,128)(2,1)} %bitcast.181), channel_id=1, source_target_pairs={{4,0},{8,4},{12,8},{16,12},{20,16},{24,20},{28,24},{5,1},{9,5},{13... | collective-permute-start | bytes 1327112 | tf_op jit(solution)/shard_map/ppermute | solution.py:16
  220.3 268.9 %collective-permute-start.21 = (bf16[1728,128]{1,0:T(8,128)(2,1)}, bf16[1728,128]{1,0:T(8,128)(2,1)}, u32[]{:S(2)}, u32[]{:S(2)}) collective-permute-start(bf16[1728,128]{1,0:T(8,128)(2,1)} %bitcast.184), channel_id=1, source_target_pairs={{1,0},{3,2},{5,4},{7,6},{9,8},{11,10},{13,12},{15,14},{17,16},{19,... | collective-permute-start | bytes 1327112 | tf_op jit(solution)/shard_map/ppermute | solution.py:16
  223.3 272.7 %collective-permute-start.19 = (bf16[1728,128]{1,0:T(8,128)(2,1)}, bf16[1728,128]{1,0:T(8,128)(2,1)}, u32[]{:S(2)}, u32[]{:S(2)}) collective-permute-start(bf16[1728,128]{1,0:T(8,128)(2,1)} %bitcast.185), channel_id=1, source_target_pairs={{0,4},{4,8},{8,12},{12,16},{16,20},{20,24},{24,28},{1,5},{5,9},{9,... | collective-permute-start | bytes 1327112 | tf_op jit(solution)/shard_map/ppermute | solution.py:11
  227.2 273.1 %collective-permute-start.20 = (bf16[1728,128]{1,0:T(8,128)(2,1)}, bf16[1728,128]{1,0:T(8,128)(2,1)}, u32[]{:S(2)}, u32[]{:S(2)}) collective-permute-start(bf16[1728,128]{1,0:T(8,128)(2,1)} %bitcast.186), channel_id=1, source_target_pairs={{4,0},{8,4},{12,8},{16,12},{20,16},{24,20},{28,24},{5,1},{9,5},{13... | collective-permute-start | bytes 1327112 | tf_op jit(solution)/shard_map/ppermute | solution.py:16
  349.9 135.6 %copy-start.6 = (bf16[1,1728,128]{2,1,0:T(8,128)(2,1)S(1)}, bf16[1,1728,128]{2,1,0:T(8,128)(2,1)}, u32[]{:S(2)}) copy-start(bf16[1,1728,128]{2,1,0:T(8,128)(2,1)} %reduce-scatter.23.cloned.1.call-done) | copy-start | bytes 1327108
  349.9 136.9 %copy-start.4 = (bf16[1,1728,128]{2,1,0:T(8,128)(2,1)S(1)}, bf16[1,1728,128]{2,1,0:T(8,128)(2,1)}, u32[]{:S(2)}) copy-start(bf16[1,1728,128]{2,1,0:T(8,128)(2,1)} %reduce-scatter.19.cloned.1.call-done) | copy-start | bytes 1327108
  349.9 141.2 %copy-start.7 = (bf16[1,1728,128]{2,1,0:T(8,128)(2,1)S(1)}, bf16[1,1728,128]{2,1,0:T(8,128)(2,1)}, u32[]{:S(2)}) copy-start(bf16[1,1728,128]{2,1,0:T(8,128)(2,1)} %reduce-scatter.21.cloned.1.call-done) | copy-start | bytes 1327108
  439.4 56.6 %copy-start.5 = (bf16[1,1728,128]{2,1,0:T(8,128)(2,1)S(1)}, bf16[1,1728,128]{2,1,0:T(8,128)(2,1)}, u32[]{:S(2)}) copy-start(bf16[1,1728,128]{2,1,0:T(8,128)(2,1)} %reduce-scatter.17.cloned.1.call-done) | copy-start | bytes 1327108
  485.5 18.8 %collective-permute-start.18 = (bf16[1728,128]{1,0:T(8,128)(2,1)S(1)}, bf16[1728,128]{1,0:T(8,128)(2,1)S(1)}, u32[]{:S(2)}, u32[]{:S(2)}) collective-permute-start(bf16[1728,128]{1,0:T(8,128)(2,1)S(1)} %bitcast.183), channel_id=1, source_target_pairs={{0,1},{2,3},{4,5},{6,7},{8,9},{10,11},{12,13},{14,15},{16,17},{18,... | collective-permute-start | bytes 1327112 | tf_op jit(solution)/shard_map/ppermute | solution.py:11
  486.8 23.9 %collective-permute-start.16 = (bf16[1728,128]{1,0:T(8,128)(2,1)S(1)}, bf16[1728,128]{1,0:T(8,128)(2,1)S(1)}, u32[]{:S(2)}, u32[]{:S(2)}) collective-permute-start(bf16[1728,128]{1,0:T(8,128)(2,1)S(1)} %bitcast.173), channel_id=1, source_target_pairs={{0,4},{4,8},{8,12},{12,16},{16,20},{20,24},{24,28},{1,5},{5,9},{9,... | collective-permute-start | bytes 1327112 | tf_op jit(solution)/shard_map/ppermute | solution.py:11
  489.2 22.8 %collective-permute-start.17 = (bf16[1728,128]{1,0:T(8,128)(2,1)S(1)}, bf16[1728,128]{1,0:T(8,128)(2,1)S(1)}, u32[]{:S(2)}, u32[]{:S(2)}) collective-permute-start(bf16[1728,128]{1,0:T(8,128)(2,1)S(1)} %bitcast.174), channel_id=1, source_target_pairs={{4,0},{8,4},{12,8},{16,12},{20,16},{24,20},{28,24},{5,1},{9,5},{13... | collective-permute-start | bytes 1327112 | tf_op jit(solution)/shard_map/ppermute | solution.py:16
  491.2 26.4 %copy-start.12 = (bf16[1728,127]{1,0:T(8,128)(2,1)S(1)}, bf16[1728,127]{1,0:T(8,128)(2,1)}, u32[]{:S(2)}) copy-start(bf16[1728,127]{1,0:T(8,128)(2,1)} %get-tuple-element.41) | copy-start | bytes 1316740
  491.2 26.4 %copy-start.13 = (bf16[1728,127]{1,0:T(8,128)(2,1)S(1)}, bf16[1728,127]{1,0:T(8,128)(2,1)}, u32[]{:S(2)}) copy-start(bf16[1728,127]{1,0:T(8,128)(2,1)} %get-tuple-element.42) | copy-start | bytes 1316740
  491.2 26.4 %copy-start.21 = (f32[1728]{0:T(1024)S(1)}, f32[1728]{0:T(1024)}, u32[]{:S(2)}) copy-start(f32[1728]{0:T(1024)} %get-tuple-element.7) | copy-start | bytes 20740
  491.2 26.4 %copy-start.22 = (f32[1728]{0:T(1024)S(1)}, f32[1728]{0:T(1024)}, u32[]{:S(2)}) copy-start(f32[1728]{0:T(1024)} %get-tuple-element.8) | copy-start | bytes 20740
  491.2 26.4 %copy-start.23 = (f32[1728]{0:T(1024)S(1)}, f32[1728]{0:T(1024)}, u32[]{:S(2)}) copy-start(f32[1728]{0:T(1024)} %get-tuple-element.9) | copy-start | bytes 20740
  491.2 26.4 %copy-start.34 = (pred[1728]{0:T(1024)(128)(4,1)S(1)}, pred[1728]{0:T(1024)(128)(4,1)}, u32[]{:S(2)}) copy-start(pred[1728]{0:T(1024)(128)(4,1)} %get-tuple-element.23) | copy-start | bytes 5188
  491.2 26.4 %copy-start.35 = (pred[1728]{0:T(1024)(128)(4,1)S(1)}, pred[1728]{0:T(1024)(128)(4,1)}, u32[]{:S(2)}) copy-start(pred[1728]{0:T(1024)(128)(4,1)} %get-tuple-element.24) | copy-start | bytes 5188
  491.2 26.4 %copy-start.36 = (pred[1728]{0:T(1024)(128)(4,1)S(1)}, pred[1728]{0:T(1024)(128)(4,1)}, u32[]{:S(2)}) copy-start(pred[1728]{0:T(1024)(128)(4,1)} %get-tuple-element.25) | copy-start | bytes 5188
  491.3 26.4 %copy-start.41 = (f32[128]{0:T(128)S(1)}, f32[128]{0:T(128)}, u32[]{:S(2)}) copy-start(f32[128]{0:T(128)} %get-tuple-element.52) | copy-start | bytes 1540
  496.0 19.7 %collective-permute-start.15 = (bf16[1728,128]{1,0:T(8,128)(2,1)S(1)}, bf16[1728,128]{1,0:T(8,128)(2,1)S(1)}, u32[]{:S(2)}, u32[]{:S(2)}) collective-permute-start(bf16[1728,128]{1,0:T(8,128)(2,1)S(1)} %bitcast.177), channel_id=1, source_target_pairs={{1,0},{3,2},{5,4},{7,6},{9,8},{11,10},{13,12},{15,14},{17,16},{19,... | collective-permute-start | bytes 1327112 | tf_op jit(solution)/shard_map/ppermute | solution.py:16
  500.3 19.7 %collective-permute-start.13 = (bf16[1728,128]{1,0:T(8,128)(2,1)S(1)}, bf16[1728,128]{1,0:T(8,128)(2,1)S(1)}, u32[]{:S(2)}, u32[]{:S(2)}) collective-permute-start(bf16[1728,128]{1,0:T(8,128)(2,1)S(1)} %bitcast.178), channel_id=1, source_target_pairs={{0,4},{4,8},{8,12},{12,16},{16,20},{20,24},{24,28},{1,5},{5,9},{9,... | collective-permute-start | bytes 1327112 | tf_op jit(solution)/shard_map/ppermute | solution.py:11
  504.3 20.1 %collective-permute-start.14 = (bf16[1728,128]{1,0:T(8,128)(2,1)S(1)}, bf16[1728,128]{1,0:T(8,128)(2,1)S(1)}, u32[]{:S(2)}, u32[]{:S(2)}) collective-permute-start(bf16[1728,128]{1,0:T(8,128)(2,1)S(1)} %bitcast.179), channel_id=1, source_target_pairs={{4,0},{8,4},{12,8},{16,12},{20,16},{24,20},{28,24},{5,1},{9,5},{13... | collective-permute-start | bytes 1327112 | tf_op jit(solution)/shard_map/ppermute | solution.py:16
  506.3 23.9 %copy-start.10 = (bf16[1728,127]{1,0:T(8,128)(2,1)S(1)}, bf16[1728,127]{1,0:T(8,128)(2,1)}, u32[]{:S(2)}) copy-start(bf16[1728,127]{1,0:T(8,128)(2,1)} %get-tuple-element.39) | copy-start | bytes 1316740
  510.7 17.6 %collective-permute-start.12 = (bf16[1728,128]{1,0:T(8,128)(2,1)S(1)}, bf16[1728,128]{1,0:T(8,128)(2,1)S(1)}, u32[]{:S(2)}, u32[]{:S(2)}) collective-permute-start(bf16[1728,128]{1,0:T(8,128)(2,1)S(1)} %bitcast.175), channel_id=1, source_target_pairs={{0,1},{2,3},{4,5},{6,7},{8,9},{10,11},{12,13},{14,15},{16,17},{18,... | collective-permute-start | bytes 1327112 | tf_op jit(solution)/shard_map/ppermute | solution.py:11
  512.0 20.4 %collective-permute-start.10 = (bf16[1728,128]{1,0:T(8,128)(2,1)S(1)}, bf16[1728,128]{1,0:T(8,128)(2,1)S(1)}, u32[]{:S(2)}, u32[]{:S(2)}) collective-permute-start(bf16[1728,128]{1,0:T(8,128)(2,1)S(1)} %bitcast.165), channel_id=1, source_target_pairs={{0,4},{4,8},{8,12},{12,16},{16,20},{20,24},{24,28},{1,5},{5,9},{9,... | collective-permute-start | bytes 1327112 | tf_op jit(solution)/shard_map/ppermute | solution.py:11
  515.7 18.1 %collective-permute-start.11 = (bf16[1728,128]{1,0:T(8,128)(2,1)S(1)}, bf16[1728,128]{1,0:T(8,128)(2,1)S(1)}, u32[]{:S(2)}, u32[]{:S(2)}) collective-permute-start(bf16[1728,128]{1,0:T(8,128)(2,1)S(1)} %bitcast.166), channel_id=1, source_target_pairs={{4,0},{8,4},{12,8},{16,12},{20,16},{24,20},{28,24},{5,1},{9,5},{13... | collective-permute-start | bytes 1327112 | tf_op jit(solution)/shard_map/ppermute | solution.py:16
  520.0 17.4 %collective-permute-start.9 = (bf16[1728,128]{1,0:T(8,128)(2,1)S(1)}, bf16[1728,128]{1,0:T(8,128)(2,1)S(1)}, u32[]{:S(2)}, u32[]{:S(2)}) collective-permute-start(bf16[1728,128]{1,0:T(8,128)(2,1)S(1)} %bitcast.169), channel_id=1, source_target_pairs={{1,0},{3,2},{5,4},{7,6},{9,8},{11,10},{13,12},{15,14},{17,16},{19,... | collective-permute-start | bytes 1327112 | tf_op jit(solution)/shard_map/ppermute | solution.py:16
  524.4 17.4 %collective-permute-start.7 = (bf16[1728,128]{1,0:T(8,128)(2,1)S(1)}, bf16[1728,128]{1,0:T(8,128)(2,1)S(1)}, u32[]{:S(2)}, u32[]{:S(2)}) collective-permute-start(bf16[1728,128]{1,0:T(8,128)(2,1)S(1)} %bitcast.170), channel_id=1, source_target_pairs={{0,4},{4,8},{8,12},{12,16},{16,20},{20,24},{24,28},{1,5},{5,9},{9,... | collective-permute-start | bytes 1327112 | tf_op jit(solution)/shard_map/ppermute | solution.py:11
  528.3 17.8 %collective-permute-start.8 = (bf16[1728,128]{1,0:T(8,128)(2,1)S(1)}, bf16[1728,128]{1,0:T(8,128)(2,1)S(1)}, u32[]{:S(2)}, u32[]{:S(2)}) collective-permute-start(bf16[1728,128]{1,0:T(8,128)(2,1)S(1)} %bitcast.171), channel_id=1, source_target_pairs={{4,0},{8,4},{12,8},{16,12},{20,16},{24,20},{28,24},{5,1},{9,5},{13... | collective-permute-start | bytes 1327112 | tf_op jit(solution)/shard_map/ppermute | solution.py:16
  532.5 17.5 %collective-permute-start.6 = (bf16[1728,128]{1,0:T(8,128)(2,1)S(1)}, bf16[1728,128]{1,0:T(8,128)(2,1)S(1)}, u32[]{:S(2)}, u32[]{:S(2)}) collective-permute-start(bf16[1728,128]{1,0:T(8,128)(2,1)S(1)} %bitcast.167), channel_id=1, source_target_pairs={{0,1},{2,3},{4,5},{6,7},{8,9},{10,11},{12,13},{14,15},{16,17},{18,... | collective-permute-start | bytes 1327112 | tf_op jit(solution)/shard_map/ppermute | solution.py:11
  533.8 20.4 %collective-permute-start.4 = (bf16[1728,128]{1,0:T(8,128)(2,1)S(1)}, bf16[1728,128]{1,0:T(8,128)(2,1)S(1)}, u32[]{:S(2)}, u32[]{:S(2)}) collective-permute-start(bf16[1728,128]{1,0:T(8,128)(2,1)S(1)} %bitcast.157), channel_id=1, source_target_pairs={{0,4},{4,8},{8,12},{12,16},{16,20},{20,24},{24,28},{1,5},{5,9},{9,... | collective-permute-start | bytes 1327112 | tf_op jit(solution)/shard_map/ppermute | solution.py:11
  537.5 18.2 %collective-permute-start.5 = (bf16[1728,128]{1,0:T(8,128)(2,1)S(1)}, bf16[1728,128]{1,0:T(8,128)(2,1)S(1)}, u32[]{:S(2)}, u32[]{:S(2)}) collective-permute-start(bf16[1728,128]{1,0:T(8,128)(2,1)S(1)} %bitcast.158), channel_id=1, source_target_pairs={{4,0},{8,4},{12,8},{16,12},{20,16},{24,20},{28,24},{5,1},{9,5},{13... | collective-permute-start | bytes 1327112 | tf_op jit(solution)/shard_map/ppermute | solution.py:16
  541.7 14.1 %collective-permute-start.3 = (bf16[1728,128]{1,0:T(8,128)(2,1)S(1)}, bf16[1728,128]{1,0:T(8,128)(2,1)S(1)}, u32[]{:S(2)}, u32[]{:S(2)}) collective-permute-start(bf16[1728,128]{1,0:T(8,128)(2,1)S(1)} %bitcast.161), channel_id=1, source_target_pairs={{1,0},{3,2},{5,4},{7,6},{9,8},{11,10},{13,12},{15,14},{17,16},{19,... | collective-permute-start | bytes 1327112 | tf_op jit(solution)/shard_map/ppermute | solution.py:16
  546.1 12.0 %collective-permute-start.1 = (bf16[1728,128]{1,0:T(8,128)(2,1)S(1)}, bf16[1728,128]{1,0:T(8,128)(2,1)S(1)}, u32[]{:S(2)}, u32[]{:S(2)}) collective-permute-start(bf16[1728,128]{1,0:T(8,128)(2,1)S(1)} %bitcast.162), channel_id=1, source_target_pairs={{0,4},{4,8},{8,12},{12,16},{16,20},{20,24},{24,28},{1,5},{5,9},{9,... | collective-permute-start | bytes 1327112 | tf_op jit(solution)/shard_map/ppermute | solution.py:11
  550.0 9.9 %collective-permute-start.2 = (bf16[1728,128]{1,0:T(8,128)(2,1)S(1)}, bf16[1728,128]{1,0:T(8,128)(2,1)S(1)}, u32[]{:S(2)}, u32[]{:S(2)}) collective-permute-start(bf16[1728,128]{1,0:T(8,128)(2,1)S(1)} %bitcast.163), channel_id=1, source_target_pairs={{4,0},{8,4},{12,8},{16,12},{20,16},{24,20},{28,24},{5,1},{9,5},{13... | collective-permute-start | bytes 1327112 | tf_op jit(solution)/shard_map/ppermute | solution.py:16
  554.2 13.9 %collective-permute-start = (bf16[1728,128]{1,0:T(8,128)(2,1)S(1)}, bf16[1728,128]{1,0:T(8,128)(2,1)S(1)}, u32[]{:S(2)}, u32[]{:S(2)}) collective-permute-start(bf16[1728,128]{1,0:T(8,128)(2,1)S(1)} %bitcast.159), channel_id=1, source_target_pairs={{0,1},{2,3},{4,5},{6,7},{8,9},{10,11},{12,13},{14,15},{16,17},{18,... | collective-permute-start | bytes 1327112 | tf_op jit(solution)/shard_map/ppermute | solution.py:11
  (31 other events, 538.2 us)
Sparse Core Ops, SparseCore 0:
  15.8 50.4 all-gather.6
  67.8 49.3 all-gather.4
  119.6 42.2 reduce-scatter.22
  164.2 42.2 reduce-scatter.20
  208.7 51.8 reduce-scatter.18
  262.9 42.3 reduce-scatter.16
  307.6 42.2 reduce-scatter.14
  352.3 42.2 reduce-scatter.12
  397.0 42.2 reduce-scatter.10
  441.6 42.2 reduce-scatter.8
where the time goes:
time: 629 us; the launch traced here: 620 us
  waiting for transfers between devices  336 us (53%)
  matrix products  102 us (16%)
  starting transfers between devices  66.9 us (11%)
  local copies, waits for them, and re-layouts  65 us (10%)
  other arithmetic  34.9 us (6%)
  between operations  14.7 us (2%)
    reduce_scatter x8, waiting for transfers between devices, on_device(): lax.psum_scatter(partial, 'vin', scatter_dimension=0, tiled=True)[0]  240 us
    dot_general x8, matrix products, on_device(): jnp.einsum('vu,zux->zvx', block, planes[row], preferred_element_type=jnp....  102 us
    all_gather x2, waiting for transfers between devices, on_device(): lax.all_gather(distribution[:, :, row, :], 'vout', axis=0, tiled=True)  85.3 us
    ppermute x12, starting transfers between devices, from_lower(): return lax.ppermute(values, axis, [(i, i + 1) for i in range(ends)])  34.4 us
    ppermute x12, starting transfers between devices, from_higher(): return lax.ppermute(values, axis, [(i + 1, i) for i in range(ends)])  31.7 us
    broadcast_in_dim x1, local copies, waits for them, and re-layouts, on_device(): return jnp.concatenate(outs, axis=0)[None]  30 us
    another operation x8, other arithmetic, on_device(): outs.append(jnp.stack(done, axis=1))  22.3 us
    slice x8, local copies, waits for them, and re-layouts, shifted(): return jnp.concatenate([edge, values[:, :-1]], axis=1)  15.4 us
  transfers between devices with their start and end apart: 34, of which 11 were waited for; matrix products, arithmetic and copies ran while one was open for 23% of the time, Pallas kernels for 0%

commit v1 on v0

--- a/solution.py
+++ b/solution.py
@@ -4,6 +4,18 @@
 from jax.sharding import PartitionSpec as P
 
 CHUNKS = 4
+
+
+def collect(array, axis, dim):
+    ways, here, step = (lax.axis_size(axis), lax.axis_index(axis), array.shape[dim])
+    line, have = (array, 1)
+    while have < ways:
+        line = jnp.concatenate(
+            [line, lax.ppermute(line, axis, [(d, (d - have) % ways) for d in range(ways)])],
+            axis=dim,
+        )
+        have = 2 * have
+    return jnp.roll(line, here * step, axis=dim)
 
 
 def from_lower(values, axis):
@@ -36,10 +48,7 @@
     rows = distribution.shape[2]
     velocities = collision.shape[0]
     chunk = velocities // CHUNKS
-    planes = [
-        lax.all_gather(distribution[:, :, row, :], "vout", axis=0, tiled=True)
-        for row in range(rows)
-    ]
+    planes = [collect(distribution[:, :, row, :], "vout", 0) for row in range(rows)]
     fluid = (1 - cell_flags[0]).astype(jnp.float32)
     relaxed = [[None] * rows for _ in range(CHUNKS)]
     for row in range(rows):

time: 629 us -> 594 us (0.944)
  waiting for transfers between devices: 336 us -> 291 us
    all_gather x2 -> x0, waiting for transfers between devices: 85.3 us -> none  [on_device(): lax.all_gather(distribution[:, :, row, :], 'vout', axis=0, tiled=True)]
    ppermute x0 -> x2, waiting for transfers between devices: none -> 76 us  [collect(): lax.ppermute(line, axis, [(d, (d - have) % ways) for d in range(ways)])]
    reduce_scatter x8, waiting for transfers between devices: 240 us -> 205 us  [on_device(): lax.psum_scatter(partial, 'vin', scatter_dimension=0, tiled=True)[0]]
  transfers between devices with their start and end apart: 34 -> 34, of which waited for: 11 -> 10; matrix products, arithmetic and copies ran while one was open for 23% -> 22% of each run, Pallas kernels for 0% -> 0%
where the time goes in v1:
time: 594 us; the launch traced here: 586 us
  waiting for transfers between devices  291 us (49%)
  matrix products  101 us (17%)
  starting transfers between devices  71.1 us (12%)
  local copies, waits for them, and re-layouts  67.3 us (11%)
  other arithmetic  41.1 us (7%)
  between operations  14.7 us (2%)
    reduce_scatter x8, waiting for transfers between devices, on_device(): lax.psum_scatter(partial, 'vin', scatter_dimension=0, tiled=True)[0]  205 us
    dot_general x8, matrix products, on_device(): jnp.einsum('vu,zux->zvx', block, planes[row], preferred_element_type=jnp....  101 us
    ppermute x2, waiting for transfers between devices, collect(): lax.ppermute(line, axis, [(d, (d - have) % ways) for d in range(ways)])  76 us
    ppermute x12, starting transfers between devices, from_lower(): return lax.ppermute(values, axis, [(i, i + 1) for i in range(ends)])  36 us
    ppermute x12, starting transfers between devices, from_higher(): return lax.ppermute(values, axis, [(i + 1, i) for i in range(ends)])  31.7 us
    broadcast_in_dim x1, local copies, waits for them, and re-layouts, on_device(): return jnp.concatenate(outs, axis=0)[None]  30 us
    another operation x8, other arithmetic, on_device(): outs.append(jnp.stack(done, axis=1))  22.3 us
    slice x8, local copies, waits for them, and re-layouts, shifted(): return jnp.concatenate([edge, values[:, :-1]], axis=1)  15.4 us
  transfers between devices with their start and end apart: 34, of which 10 were waited for; matrix products, arithmetic and copies ran while one was open for 22% of the time, Pallas kernels for 0%

profile of v1, /device:TPU:13, one launch (start us, length us, event | category | flops | bytes accessed | tf_op | source)
XLA Modules:
  0.0 586.4 jit_solution(3161544754090907885)
XLA Ops:
  6.5 7.7 %fusion.142 = (bf16[4,1728,1,128]{3,2,1,0:T(2,128)(2,1)S(1)}, bf16[4,1728,1,128]{3,2,1,0:T(2,128)(2,1)S(1)}) fusion(bf16[4,1728,2,128]{3,2,1,0:T(2,128)(2,1)} %param.7), kind=kLoop, calls=%fused_computation.184 | loop fusion | bytes 7077888 | tf_op jit(solution)/shard_map/slice | solution.py:51
  16.9 38.6 %collective-permute-done.1 = bf16[4,1728,128]{2,1,0:T(8,128)(2,1)} collective-permute-done((bf16[4,1728,128]{2,1,0:T(8,128)(2,1)}, bf16[4,1728,128]{2,1,0:T(8,128)(2,1)}, u32[]{:S(2)}, u32[]{:S(2)}) %collective-permute-start.1) | collective-permute-done | bytes 1769504 | tf_op jit(solution)/shard_map/ppermute | solution.py:14
  55.4 3.8 fusion.49
  61.0 14.1 %fusion.54 = bf16[8,1728,128]{2,1,0:T(8,128)(2,1)} fusion(bf16[8,1728,128]{2,1,0:T(8,128)(2,1)S(1)} %fusion.49, bf16[6912,1728]{0,1:T(8,128)(2,1)} %param.8), kind=kOutput, calls=%fused_computation.47 | convolution fusion | flops 6117064704 | bytes 13271040 | tf_op jit(solution)/shard_map/vu,zux->zvx/dot_general | solution.py:57
  76.9 37.5 %collective-permute-done = bf16[4,1728,128]{2,1,0:T(8,128)(2,1)S(1)} collective-permute-done((bf16[4,1728,128]{2,1,0:T(8,128)(2,1)S(1)}, bf16[4,1728,128]{2,1,0:T(8,128)(2,1)S(1)}, u32[]{:S(2)}, u32[]{:S(2)}) %collective-permute-start) | collective-permute-done | bytes 1769504 | tf_op jit(solution)/shard_map/ppermute | solution.py:14
  114.3 2.4 fusion.52
  118.5 14.1 %fusion.57 = bf16[8,1728,128]{2,1,0:T(8,128)(2,1)} fusion(bf16[8,1728,128]{2,1,0:T(8,128)(2,1)S(1)} %fusion.52, bf16[6912,1728]{0,1:T(8,128)(2,1)} %param.8), kind=kOutput, calls=%fused_computation.48 | convolution fusion | flops 6117064704 | bytes 13271040 | tf_op jit(solution)/shard_map/vu,zux->zvx/dot_general | solution.py:57
  134.6 10.8 %fusion.60 = bf16[8,1728,128]{2,1,0:T(8,128)(2,1)} fusion(bf16[8,1728,128]{2,1,0:T(8,128)(2,1)S(1)} %copy-done.9, bf16[6912,1728]{0,1:T(8,128)(2,1)} %param.8), kind=kOutput, calls=%fused_computation.49 | convolution fusion | flops 6117064704 | bytes 13271040 | tf_op jit(solution)/shard_map/vu,zux->zvx/dot_general | solution.py:57
  145.7 11.5 %fusion.63 = bf16[8,1728,128]{2,1,0:T(8,128)(2,1)} fusion(bf16[8,1728,128]{2,1,0:T(8,128)(2,1)} %copy-done.10, bf16[6912,1728]{0,1:T(8,128)(2,1)} %param.8), kind=kOutput, calls=%fused_computation.50 | convolution fusion | flops 6117064704 | bytes 13271040 | tf_op jit(solution)/shard_map/vu,zux->zvx/dot_general | solution.py:57
  157.2 14.2 %fusion.66 = bf16[8,1728,128]{2,1,0:T(8,128)(2,1)} fusion(bf16[8,1728,128]{2,1,0:T(8,128)(2,1)S(1)} %copy-done.9, bf16[6912,1728]{0,1:T(8,128)(2,1)} %param.8), kind=kOutput, calls=%fused_computation.51 | convolution fusion | flops 6117064704 | bytes 13271040 | tf_op jit(solution)/shard_map/vu,zux->zvx/dot_general | solution.py:57
  171.8 14.7 %fusion.69 = bf16[8,1728,128]{2,1,0:T(8,128)(2,1)} fusion(bf16[8,1728,128]{2,1,0:T(8,128)(2,1)} %copy-done.10, bf16[6912,1728]{0,1:T(8,128)(2,1)} %param.8), kind=kOutput, calls=%fused_computation.52 | convolution fusion | flops 6117064704 | bytes 13271040 | tf_op jit(solution)/shard_map/vu,zux->zvx/dot_general | solution.py:57
  186.6 10.9 %fusion.72 = bf16[8,1728,128]{2,1,0:T(8,128)(2,1)} fusion(bf16[8,1728,128]{2,1,0:T(8,128)(2,1)S(1)} %copy-done.9, bf16[6912,1728]{0,1:T(8,128)(2,1)} %param.8), kind=kOutput, calls=%fused_computation.53 | convolution fusion | flops 6117064704 | bytes 13271040 | tf_op jit(solution)/shard_map/vu,zux->zvx/dot_general | solution.py:57
  199.6 10.9 %fusion.75 = bf16[8,1728,128]{2,1,0:T(8,128)(2,1)} fusion(bf16[8,1728,128]{2,1,0:T(8,128)(2,1)S(1)} %copy-done.11, bf16[6912,1728]{0,1:T(8,128)(2,1)} %param.8), kind=kOutput, calls=%fused_computation.54 | convolution fusion | flops 6117064704 | bytes 13271040 | tf_op jit(solution)/shard_map/vu,zux->zvx/dot_general | solution.py:57
  215.6 5.4 collective-permute-start.24
  222.9 2.9 collective-permute-start.23
  225.9 3.9 collective-permute-start.21
  229.8 2.4 collective-permute-start.22
  232.2 2.2 fusion.150
  234.4 2.3 fusion.149
  236.7 2.2 fusion.148
  238.9 33.1 %reduce-scatter.17.cloned.1.call-done = bf16[1,1728,128]{2,1,0:T(8,128)(2,1)} async-done(((bf16[8,1728,128]{2,1,0:T(8,128)(2,1)}), bf16[1,1728,128]{2,1,0:T(8,128)(2,1)}) %reduce-scatter.17.cloned.1.call-update) | async-done | bytes 442384 | tf_op jit(solution)/shard_map/reduce_scatter | solution.py:60
  272.0 2.2 fusion.147
  274.2 42.3 %reduce-scatter.15.cloned.1.call-done = bf16[1,1728,128]{2,1,0:T(8,128)(2,1)} async-done(((bf16[8,1728,128]{2,1,0:T(8,128)(2,1)}), bf16[1,1728,128]{2,1,0:T(8,128)(2,1)}) %reduce-scatter.15.cloned.1.call-update) | async-done | bytes 442384 | tf_op jit(solution)/shard_map/reduce_scatter | solution.py:60
  316.5 2.3 fusion.146
  318.9 42.3 %reduce-scatter.13.cloned.1.call-done = bf16[1,1728,128]{2,1,0:T(8,128)(2,1)} async-done(((bf16[8,1728,128]{2,1,0:T(8,128)(2,1)}), bf16[1,1728,128]{2,1,0:T(8,128)(2,1)}) %reduce-scatter.13.cloned.1.call-update) | async-done | bytes 442384 | tf_op jit(solution)/shard_map/reduce_scatter | solution.py:60
  362.5 43.4 %reduce-scatter.11.cloned.1.call-done = bf16[1,1728,128]{2,1,0:T(8,128)(2,1)} async-done(((bf16[8,1728,128]{2,1,0:T(8,128)(2,1)}), bf16[1,1728,128]{2,1,0:T(8,128)(2,1)}) %reduce-scatter.11.cloned.1.call-update) | async-done | bytes 442384 | tf_op jit(solution)/shard_map/reduce_scatter | solution.py:60
  407.3 43.4 %reduce-scatter.9.cloned.1.call-done = bf16[1,1728,128]{2,1,0:T(8,128)(2,1)} async-done(((bf16[8,1728,128]{2,1,0:T(8,128)(2,1)}), bf16[1,1728,128]{2,1,0:T(8,128)(2,1)}) %reduce-scatter.9.cloned.1.call-update) | async-done | bytes 442384 | tf_op jit(solution)/shard_map/reduce_scatter | solution.py:60
  453.5 2.3 collective-permute-start.18
  455.8 2.0 collective-permute-start.19
  458.0 4.7 fusion.134
  462.7 4.2 collective-permute-start.17
  467.0 3.9 collective-permute-start.15
  473.0 4.4 fusion.135
  478.6 3.6 collective-permute-start.12
  484.4 2.2 fusion.136
  486.6 4.3 collective-permute-start.11
  491.0 3.9 collective-permute-start.9
  496.9 2.2 fusion.137
  500.4 3.6 collective-permute-start.6
  506.1 2.2 fusion.138
  508.4 4.3 collective-permute-start.5
  512.7 3.9 collective-permute-start.3
  518.6 2.2 fusion.139
  522.4 2.2 fusion.140
  526.6 8.0 %collective-permute-done.2 = bf16[1728,128]{1,0:T(8,128)(2,1)S(1)} collective-permute-done((bf16[1728,128]{1,0:T(8,128)(2,1)S(1)}, bf16[1728,128]{1,0:T(8,128)(2,1)S(1)}, u32[]{:S(2)}, u32[]{:S(2)}) %collective-permute-start.2) | collective-permute-done | bytes 442400 | tf_op jit(solution)/shard_map/ppermute | solution.py:23
  534.6 2.2 fusion.141
  536.8 12.5 %maximum_bitcast_fusion = bf16[1,6912,2,128]{3,1,2,0:T(8,128)(2,1)S(1)} fusion(bf16[1728,1,128]{2,0,1:T(8,128)(2,1)S(1)} %fusion.134, bf16[1728,1,128]{2,0,1:T(8,128)(2,1)S(1)} %fusion.135, bf16[1728,1,128]{2,0,1:T(8,128)(2,1)S(1)} %fusion.136, bf16[1728,1,128]{2,0,1:T(8,128)(2,1)S(1)} %fusion.137, bf16[1728,1,128]{2,0,1:T(8,128)(2,1)S(1)} %fusion.138, ...), kind=kLoop, calls=%fused_computation.46 | loop fusion | flops 28311552 | bytes 7077888 | tf_op jit(solution)/shard_map/broadcast_in_dim | solution.py:82
  549.3 30.0 %copy.12 = bf16[1,6912,2,128]{3,2,1,0:T(2,128)(2,1)} copy(bf16[1,6912,2,128]{3,1,2,0:T(8,128)(2,1)S(1)} %maximum_bitcast_fusion) | data formatting | bytes 7077888 | tf_op jit(solution)/shard_map/broadcast_in_dim | solution.py:82
  (161 shorter events, 41.0 us)
Async XLA Ops:
  6.5 209.1 %reduce-scatter.23.cloned.1.call-start = ((), (), s32[]{:S(2)}) async-start(), calls=%async_computation.15 | async-start | bytes 3981312 | tf_op jit(solution)/shard_map/reduce_scatter | solution.py:60
  15.7 39.8 %collective-permute-start.1 = (bf16[4,1728,128]{2,1,0:T(8,128)(2,1)}, bf16[4,1728,128]{2,1,0:T(8,128)(2,1)}, u32[]{:S(2)}, u32[]{:S(2)}) collective-permute-start(bf16[4,1728,128]{2,1,0:T(8,128)(2,1)} %bitcast.134), channel_id=1, source_target_pairs={{0,2},{2,0},{1,3},{3,1},{4,6},{6,4},{5,7},{7,5},{8,10},{10,8},{9,1... | collective-permute-start | bytes 5308424 | tf_op jit(solution)/shard_map/ppermute | solution.py:14
  75.1 147.8 %reduce-scatter.21.cloned.1.call-start = ((), (), s32[]{:S(2)}) async-start(), calls=%async_computation.14 | async-start | bytes 3981312 | tf_op jit(solution)/shard_map/reduce_scatter | solution.py:60
  75.6 38.7 %collective-permute-start = (bf16[4,1728,128]{2,1,0:T(8,128)(2,1)S(1)}, bf16[4,1728,128]{2,1,0:T(8,128)(2,1)S(1)}, u32[]{:S(2)}, u32[]{:S(2)}) collective-permute-start(bf16[4,1728,128]{2,1,0:T(8,128)(2,1)S(1)} %bitcast.136), channel_id=1, source_target_pairs={{0,2},{2,0},{1,3},{3,1},{4,6},{6,4},{5,7},{7,5},{8,10},{10,8},{9,1... | collective-permute-start | bytes 5308424 | tf_op jit(solution)/shard_map/ppermute | solution.py:14
  132.6 104.0 %reduce-scatter.19.cloned.1.call-start = ((), (), s32[]{:S(2)}) async-start(), calls=%async_computation.13 | async-start | bytes 3981312 | tf_op jit(solution)/shard_map/reduce_scatter | solution.py:60
  145.4 126.6 %reduce-scatter.17.cloned.1.call-start = ((), (), s32[]{:S(2)}) async-start(), calls=%async_computation.12 | async-start | bytes 3981312 | tf_op jit(solution)/shard_map/reduce_scatter | solution.py:60
  157.2 159.3 %reduce-scatter.15.cloned.1.call-start = ((), (), s32[]{:S(2)}) async-start(), calls=%async_computation.11 | async-start | bytes 3981312 | tf_op jit(solution)/shard_map/reduce_scatter | solution.py:60
  171.5 189.7 %reduce-scatter.13.cloned.1.call-start = ((), (), s32[]{:S(2)}) async-start(), calls=%async_computation.10 | async-start | bytes 3981312 | tf_op jit(solution)/shard_map/reduce_scatter | solution.py:60
  186.5 219.4 %reduce-scatter.11.cloned.1.call-start = ((), (), s32[]{:S(2)}) async-start(), calls=%async_computation.9 | async-start | bytes 3981312 | tf_op jit(solution)/shard_map/reduce_scatter | solution.py:60
  197.6 253.2 %reduce-scatter.9.cloned.1.call-start = ((), (), s32[]{:S(2)}) async-start(), calls=%async_computation.8 | async-start | bytes 3981312 | tf_op jit(solution)/shard_map/reduce_scatter | solution.py:60
  215.6 236.6 %collective-permute-start.24 = (bf16[1728,128]{1,0:T(8,128)(2,1)}, bf16[1728,128]{1,0:T(8,128)(2,1)}, u32[]{:S(2)}, u32[]{:S(2)}) collective-permute-start(bf16[1728,128]{1,0:T(8,128)(2,1)} %bitcast.162), channel_id=1, source_target_pairs={{0,4},{4,8},{8,12},{12,16},{16,20},{20,24},{24,28},{1,5},{5,9},{9,... | collective-permute-start | bytes 1327112 | tf_op jit(solution)/shard_map/ppermute | solution.py:23
  221.0 232.5 %collective-permute-start.25 = (bf16[1728,128]{1,0:T(8,128)(2,1)}, bf16[1728,128]{1,0:T(8,128)(2,1)}, u32[]{:S(2)}, u32[]{:S(2)}) collective-permute-start(bf16[1728,128]{1,0:T(8,128)(2,1)} %bitcast.163), channel_id=1, source_target_pairs={{4,0},{8,4},{12,8},{16,12},{20,16},{24,20},{28,24},{5,1},{9,5},{13... | collective-permute-start | bytes 1327112 | tf_op jit(solution)/shard_map/ppermute | solution.py:28
  222.9 232.9 %collective-permute-start.23 = (bf16[1728,128]{1,0:T(8,128)(2,1)}, bf16[1728,128]{1,0:T(8,128)(2,1)}, u32[]{:S(2)}, u32[]{:S(2)}) collective-permute-start(bf16[1728,128]{1,0:T(8,128)(2,1)} %bitcast.166), channel_id=1, source_target_pairs={{1,0},{3,2},{5,4},{7,6},{9,8},{11,10},{13,12},{15,14},{17,16},{19,... | collective-permute-start | bytes 1327112 | tf_op jit(solution)/shard_map/ppermute | solution.py:28
  225.9 236.8 %collective-permute-start.21 = (bf16[1728,128]{1,0:T(8,128)(2,1)}, bf16[1728,128]{1,0:T(8,128)(2,1)}, u32[]{:S(2)}, u32[]{:S(2)}) collective-permute-start(bf16[1728,128]{1,0:T(8,128)(2,1)} %bitcast.167), channel_id=1, source_target_pairs={{0,4},{4,8},{8,12},{12,16},{16,20},{20,24},{24,28},{1,5},{5,9},{9,... | collective-permute-start | bytes 1327112 | tf_op jit(solution)/shard_map/ppermute | solution.py:23
  229.8 237.2 %collective-permute-start.22 = (bf16[1728,128]{1,0:T(8,128)(2,1)}, bf16[1728,128]{1,0:T(8,128)(2,1)}, u32[]{:S(2)}, u32[]{:S(2)}) collective-permute-start(bf16[1728,128]{1,0:T(8,128)(2,1)} %bitcast.168), channel_id=1, source_target_pairs={{4,0},{8,4},{12,8},{16,12},{20,16},{24,20},{28,24},{5,1},{9,5},{13... | collective-permute-start | bytes 1327112 | tf_op jit(solution)/shard_map/ppermute | solution.py:28
  316.5 135.6 %copy-start.6 = (bf16[1,1728,128]{2,1,0:T(8,128)(2,1)S(1)}, bf16[1,1728,128]{2,1,0:T(8,128)(2,1)}, u32[]{:S(2)}) copy-start(bf16[1,1728,128]{2,1,0:T(8,128)(2,1)} %reduce-scatter.23.cloned.1.call-done) | copy-start | bytes 1327108
  316.5 137.0 %copy-start.4 = (bf16[1,1728,128]{2,1,0:T(8,128)(2,1)S(1)}, bf16[1,1728,128]{2,1,0:T(8,128)(2,1)}, u32[]{:S(2)}) copy-start(bf16[1,1728,128]{2,1,0:T(8,128)(2,1)} %reduce-scatter.19.cloned.1.call-done) | copy-start | bytes 1327108
  316.5 141.3 %copy-start.7 = (bf16[1,1728,128]{2,1,0:T(8,128)(2,1)S(1)}, bf16[1,1728,128]{2,1,0:T(8,128)(2,1)}, u32[]{:S(2)}) copy-start(bf16[1,1728,128]{2,1,0:T(8,128)(2,1)} %reduce-scatter.21.cloned.1.call-done) | copy-start | bytes 1327108
  405.9 56.8 %copy-start.5 = (bf16[1,1728,128]{2,1,0:T(8,128)(2,1)S(1)}, bf16[1,1728,128]{2,1,0:T(8,128)(2,1)}, u32[]{:S(2)}) copy-start(bf16[1,1728,128]{2,1,0:T(8,128)(2,1)} %reduce-scatter.17.cloned.1.call-done) | copy-start | bytes 1327108
  452.2 18.7 %collective-permute-start.20 = (bf16[1728,128]{1,0:T(8,128)(2,1)S(1)}, bf16[1728,128]{1,0:T(8,128)(2,1)S(1)}, u32[]{:S(2)}, u32[]{:S(2)}) collective-permute-start(bf16[1728,128]{1,0:T(8,128)(2,1)S(1)} %bitcast.165), channel_id=1, source_target_pairs={{0,1},{2,3},{4,5},{6,7},{8,9},{10,11},{12,13},{14,15},{16,17},{18,... | collective-permute-start | bytes 1327112 | tf_op jit(solution)/shard_map/ppermute | solution.py:23
  453.5 23.8 %collective-permute-start.18 = (bf16[1728,128]{1,0:T(8,128)(2,1)S(1)}, bf16[1728,128]{1,0:T(8,128)(2,1)S(1)}, u32[]{:S(2)}, u32[]{:S(2)}) collective-permute-start(bf16[1728,128]{1,0:T(8,128)(2,1)S(1)} %bitcast.155), channel_id=1, source_target_pairs={{0,4},{4,8},{8,12},{12,16},{16,20},{20,24},{24,28},{1,5},{5,9},{9,... | collective-permute-start | bytes 1327112 | tf_op jit(solution)/shard_map/ppermute | solution.py:23
  455.8 22.8 %collective-permute-start.19 = (bf16[1728,128]{1,0:T(8,128)(2,1)S(1)}, bf16[1728,128]{1,0:T(8,128)(2,1)S(1)}, u32[]{:S(2)}, u32[]{:S(2)}) collective-permute-start(bf16[1728,128]{1,0:T(8,128)(2,1)S(1)} %bitcast.156), channel_id=1, source_target_pairs={{4,0},{8,4},{12,8},{16,12},{20,16},{24,20},{28,24},{5,1},{9,5},{13... | collective-permute-start | bytes 1327112 | tf_op jit(solution)/shard_map/ppermute | solution.py:28
  457.9 26.4 %copy-start.16 = (bf16[1728,127]{1,0:T(8,128)(2,1)S(1)}, bf16[1728,127]{1,0:T(8,128)(2,1)}, u32[]{:S(2)}) copy-start(bf16[1728,127]{1,0:T(8,128)(2,1)} %get-tuple-element.42) | copy-start | bytes 1316740
  457.9 26.4 %copy-start.17 = (bf16[1728,127]{1,0:T(8,128)(2,1)S(1)}, bf16[1728,127]{1,0:T(8,128)(2,1)}, u32[]{:S(2)}) copy-start(bf16[1728,127]{1,0:T(8,128)(2,1)} %get-tuple-element.43) | copy-start | bytes 1316740
  457.9 26.4 %copy-start.25 = (f32[1728]{0:T(1024)S(1)}, f32[1728]{0:T(1024)}, u32[]{:S(2)}) copy-start(f32[1728]{0:T(1024)} %get-tuple-element.8) | copy-start | bytes 20740
  457.9 26.4 %copy-start.26 = (f32[1728]{0:T(1024)S(1)}, f32[1728]{0:T(1024)}, u32[]{:S(2)}) copy-start(f32[1728]{0:T(1024)} %get-tuple-element.9) | copy-start | bytes 20740
  457.9 26.4 %copy-start.27 = (f32[1728]{0:T(1024)S(1)}, f32[1728]{0:T(1024)}, u32[]{:S(2)}) copy-start(f32[1728]{0:T(1024)} %get-tuple-element.10) | copy-start | bytes 20740
  457.9 26.4 %copy-start.38 = (pred[1728]{0:T(1024)(128)(4,1)S(1)}, pred[1728]{0:T(1024)(128)(4,1)}, u32[]{:S(2)}) copy-start(pred[1728]{0:T(1024)(128)(4,1)} %get-tuple-element.24) | copy-start | bytes 5188
  457.9 26.4 %copy-start.39 = (pred[1728]{0:T(1024)(128)(4,1)S(1)}, pred[1728]{0:T(1024)(128)(4,1)}, u32[]{:S(2)}) copy-start(pred[1728]{0:T(1024)(128)(4,1)} %get-tuple-element.25) | copy-start | bytes 5188
  457.9 26.4 %copy-start.40 = (pred[1728]{0:T(1024)(128)(4,1)S(1)}, pred[1728]{0:T(1024)(128)(4,1)}, u32[]{:S(2)}) copy-start(pred[1728]{0:T(1024)(128)(4,1)} %get-tuple-element.26) | copy-start | bytes 5188
  458.0 26.4 %copy-start.45 = (f32[128]{0:T(128)S(1)}, f32[128]{0:T(128)}, u32[]{:S(2)}) copy-start(f32[128]{0:T(128)} %get-tuple-element.53) | copy-start | bytes 1540
  462.7 19.6 %collective-permute-start.17 = (bf16[1728,128]{1,0:T(8,128)(2,1)S(1)}, bf16[1728,128]{1,0:T(8,128)(2,1)S(1)}, u32[]{:S(2)}, u32[]{:S(2)}) collective-permute-start(bf16[1728,128]{1,0:T(8,128)(2,1)S(1)} %bitcast.159), channel_id=1, source_target_pairs={{1,0},{3,2},{5,4},{7,6},{9,8},{11,10},{13,12},{15,14},{17,16},{19,... | collective-permute-start | bytes 1327112 | tf_op jit(solution)/shard_map/ppermute | solution.py:28
  467.0 19.7 %collective-permute-start.15 = (bf16[1728,128]{1,0:T(8,128)(2,1)S(1)}, bf16[1728,128]{1,0:T(8,128)(2,1)S(1)}, u32[]{:S(2)}, u32[]{:S(2)}) collective-permute-start(bf16[1728,128]{1,0:T(8,128)(2,1)S(1)} %bitcast.160), channel_id=1, source_target_pairs={{0,4},{4,8},{8,12},{12,16},{16,20},{20,24},{24,28},{1,5},{5,9},{9,... | collective-permute-start | bytes 1327112 | tf_op jit(solution)/shard_map/ppermute | solution.py:23
  470.9 20.1 %collective-permute-start.16 = (bf16[1728,128]{1,0:T(8,128)(2,1)S(1)}, bf16[1728,128]{1,0:T(8,128)(2,1)S(1)}, u32[]{:S(2)}, u32[]{:S(2)}) collective-permute-start(bf16[1728,128]{1,0:T(8,128)(2,1)S(1)} %bitcast.161), channel_id=1, source_target_pairs={{4,0},{8,4},{12,8},{16,12},{20,16},{24,20},{28,24},{5,1},{9,5},{13... | collective-permute-start | bytes 1327112 | tf_op jit(solution)/shard_map/ppermute | solution.py:28
  472.9 23.9 %copy-start.14 = (bf16[1728,127]{1,0:T(8,128)(2,1)S(1)}, bf16[1728,127]{1,0:T(8,128)(2,1)}, u32[]{:S(2)}) copy-start(bf16[1728,127]{1,0:T(8,128)(2,1)} %get-tuple-element.40) | copy-start | bytes 1316740
  477.3 17.6 %collective-permute-start.14 = (bf16[1728,128]{1,0:T(8,128)(2,1)S(1)}, bf16[1728,128]{1,0:T(8,128)(2,1)S(1)}, u32[]{:S(2)}, u32[]{:S(2)}) collective-permute-start(bf16[1728,128]{1,0:T(8,128)(2,1)S(1)} %bitcast.157), channel_id=1, source_target_pairs={{0,1},{2,3},{4,5},{6,7},{8,9},{10,11},{12,13},{14,15},{16,17},{18,... | collective-permute-start | bytes 1327112 | tf_op jit(solution)/shard_map/ppermute | solution.py:23
  478.6 20.4 %collective-permute-start.12 = (bf16[1728,128]{1,0:T(8,128)(2,1)S(1)}, bf16[1728,128]{1,0:T(8,128)(2,1)S(1)}, u32[]{:S(2)}, u32[]{:S(2)}) collective-permute-start(bf16[1728,128]{1,0:T(8,128)(2,1)S(1)} %bitcast.147), channel_id=1, source_target_pairs={{0,4},{4,8},{8,12},{12,16},{16,20},{20,24},{24,28},{1,5},{5,9},{9,... | collective-permute-start | bytes 1327112 | tf_op jit(solution)/shard_map/ppermute | solution.py:23
  482.3 18.1 %collective-permute-start.13 = (bf16[1728,128]{1,0:T(8,128)(2,1)S(1)}, bf16[1728,128]{1,0:T(8,128)(2,1)S(1)}, u32[]{:S(2)}, u32[]{:S(2)}) collective-permute-start(bf16[1728,128]{1,0:T(8,128)(2,1)S(1)} %bitcast.148), channel_id=1, source_target_pairs={{4,0},{8,4},{12,8},{16,12},{20,16},{24,20},{28,24},{5,1},{9,5},{13... | collective-permute-start | bytes 1327112 | tf_op jit(solution)/shard_map/ppermute | solution.py:28
  486.6 17.4 %collective-permute-start.11 = (bf16[1728,128]{1,0:T(8,128)(2,1)S(1)}, bf16[1728,128]{1,0:T(8,128)(2,1)S(1)}, u32[]{:S(2)}, u32[]{:S(2)}) collective-permute-start(bf16[1728,128]{1,0:T(8,128)(2,1)S(1)} %bitcast.151), channel_id=1, source_target_pairs={{1,0},{3,2},{5,4},{7,6},{9,8},{11,10},{13,12},{15,14},{17,16},{19,... | collective-permute-start | bytes 1327112 | tf_op jit(solution)/shard_map/ppermute | solution.py:28
  491.0 17.4 %collective-permute-start.9 = (bf16[1728,128]{1,0:T(8,128)(2,1)S(1)}, bf16[1728,128]{1,0:T(8,128)(2,1)S(1)}, u32[]{:S(2)}, u32[]{:S(2)}) collective-permute-start(bf16[1728,128]{1,0:T(8,128)(2,1)S(1)} %bitcast.152), channel_id=1, source_target_pairs={{0,4},{4,8},{8,12},{12,16},{16,20},{20,24},{24,28},{1,5},{5,9},{9,... | collective-permute-start | bytes 1327112 | tf_op jit(solution)/shard_map/ppermute | solution.py:23
  494.9 17.8 %collective-permute-start.10 = (bf16[1728,128]{1,0:T(8,128)(2,1)S(1)}, bf16[1728,128]{1,0:T(8,128)(2,1)S(1)}, u32[]{:S(2)}, u32[]{:S(2)}) collective-permute-start(bf16[1728,128]{1,0:T(8,128)(2,1)S(1)} %bitcast.153), channel_id=1, source_target_pairs={{4,0},{8,4},{12,8},{16,12},{20,16},{24,20},{28,24},{5,1},{9,5},{13... | collective-permute-start | bytes 1327112 | tf_op jit(solution)/shard_map/ppermute | solution.py:28
  499.1 17.5 %collective-permute-start.8 = (bf16[1728,128]{1,0:T(8,128)(2,1)S(1)}, bf16[1728,128]{1,0:T(8,128)(2,1)S(1)}, u32[]{:S(2)}, u32[]{:S(2)}) collective-permute-start(bf16[1728,128]{1,0:T(8,128)(2,1)S(1)} %bitcast.149), channel_id=1, source_target_pairs={{0,1},{2,3},{4,5},{6,7},{8,9},{10,11},{12,13},{14,15},{16,17},{18,... | collective-permute-start | bytes 1327112 | tf_op jit(solution)/shard_map/ppermute | solution.py:23
  500.4 20.4 %collective-permute-start.6 = (bf16[1728,128]{1,0:T(8,128)(2,1)S(1)}, bf16[1728,128]{1,0:T(8,128)(2,1)S(1)}, u32[]{:S(2)}, u32[]{:S(2)}) collective-permute-start(bf16[1728,128]{1,0:T(8,128)(2,1)S(1)} %bitcast.139), channel_id=1, source_target_pairs={{0,4},{4,8},{8,12},{12,16},{16,20},{20,24},{24,28},{1,5},{5,9},{9,... | collective-permute-start | bytes 1327112 | tf_op jit(solution)/shard_map/ppermute | solution.py:23
  504.1 18.2 %collective-permute-start.7 = (bf16[1728,128]{1,0:T(8,128)(2,1)S(1)}, bf16[1728,128]{1,0:T(8,128)(2,1)S(1)}, u32[]{:S(2)}, u32[]{:S(2)}) collective-permute-start(bf16[1728,128]{1,0:T(8,128)(2,1)S(1)} %bitcast.140), channel_id=1, source_target_pairs={{4,0},{8,4},{12,8},{16,12},{20,16},{24,20},{28,24},{5,1},{9,5},{13... | collective-permute-start | bytes 1327112 | tf_op jit(solution)/shard_map/ppermute | solution.py:28
  508.4 14.0 %collective-permute-start.5 = (bf16[1728,128]{1,0:T(8,128)(2,1)S(1)}, bf16[1728,128]{1,0:T(8,128)(2,1)S(1)}, u32[]{:S(2)}, u32[]{:S(2)}) collective-permute-start(bf16[1728,128]{1,0:T(8,128)(2,1)S(1)} %bitcast.143), channel_id=1, source_target_pairs={{1,0},{3,2},{5,4},{7,6},{9,8},{11,10},{13,12},{15,14},{17,16},{19,... | collective-permute-start | bytes 1327112 | tf_op jit(solution)/shard_map/ppermute | solution.py:28
  512.7 11.9 %collective-permute-start.3 = (bf16[1728,128]{1,0:T(8,128)(2,1)S(1)}, bf16[1728,128]{1,0:T(8,128)(2,1)S(1)}, u32[]{:S(2)}, u32[]{:S(2)}) collective-permute-start(bf16[1728,128]{1,0:T(8,128)(2,1)S(1)} %bitcast.144), channel_id=1, source_target_pairs={{0,4},{4,8},{8,12},{12,16},{16,20},{20,24},{24,28},{1,5},{5,9},{9,... | collective-permute-start | bytes 1327112 | tf_op jit(solution)/shard_map/ppermute | solution.py:23
  516.6 9.9 %collective-permute-start.4 = (bf16[1728,128]{1,0:T(8,128)(2,1)S(1)}, bf16[1728,128]{1,0:T(8,128)(2,1)S(1)}, u32[]{:S(2)}, u32[]{:S(2)}) collective-permute-start(bf16[1728,128]{1,0:T(8,128)(2,1)S(1)} %bitcast.145), channel_id=1, source_target_pairs={{4,0},{8,4},{12,8},{16,12},{20,16},{24,20},{28,24},{5,1},{9,5},{13... | collective-permute-start | bytes 1327112 | tf_op jit(solution)/shard_map/ppermute | solution.py:28
  520.8 13.8 %collective-permute-start.2 = (bf16[1728,128]{1,0:T(8,128)(2,1)S(1)}, bf16[1728,128]{1,0:T(8,128)(2,1)S(1)}, u32[]{:S(2)}, u32[]{:S(2)}) collective-permute-start(bf16[1728,128]{1,0:T(8,128)(2,1)S(1)} %bitcast.141), channel_id=1, source_target_pairs={{0,1},{2,3},{4,5},{6,7},{8,9},{10,11},{12,13},{14,15},{16,17},{18,... | collective-permute-start | bytes 1327112 | tf_op jit(solution)/shard_map/ppermute | solution.py:23
  (33 other events, 540.4 us)
Sparse Core Ops, SparseCore 0:
  75.3 44.2 reduce-scatter.22
  132.8 45.0 reduce-scatter.20
  180.2 42.3 reduce-scatter.18
  224.9 47.0 reduce-scatter.16
  274.2 42.3 reduce-scatter.14
  318.8 42.3 reduce-scatter.12
  363.5 42.3 reduce-scatter.10
  408.3 42.3 reduce-scatter.8
